TPU v7x, 32 devices: a whole 2x2x4 slice. The times are simulated.
32 devices in a mesh: tok: 4 (over z), hid: 8 (over y, x, core).
Axes of the slice: x: 2, y: 2, z: 4, core: 2. Of those that a mesh axis runs over, the one named last changes fastest.
Arguments:
- out_grad: bfloat16 [1024, 8192], P('hid', 'tok'), may hold values from -6 to 6
- gate_act: bfloat16 [1024, 28672], P('tok', 'hid'), may hold values from -8 to 8
- up_act: bfloat16 [1024, 28672], P('tok', 'hid'), may hold values from -6 to 6
- gate_weight: bfloat16 [8192, 28672], P('tok', 'hid'), may hold values from -0.0625 to 0.0625
- up_weight: bfloat16 [8192, 28672], P('tok', 'hid'), may hold values from -0.0625 to 0.0625
- down_weight: bfloat16 [28672, 8192], P('hid', 'tok'), may hold values from -0.03125 to 0.03125
Outputs:
- input_grad: bfloat16 [1024, 8192], P('hid', 'tok')
All inputs are finite; a program needn't handle non-finite values.
Results may differ from a plain program's by a relative error of at most 0.005.
Values may be sent and summed in bfloat16 or wider, within the bound.
A program may use at most 128 MiB of HBM per device.

v0:
```python
import math

import jax
import jax.numpy as jnp
from jax import lax
from jax.sharding import PartitionSpec as P


def swapped(x, axis, bit):
    return lax.ppermute(x, axis, [(i, i ^ 1 << bit) for i in range(lax.axis_size(axis))])


def contract_rows(left, right):
    return lax.dot_general(
        left, right, (((1,), (1,)), ((), ())), preferred_element_type=jnp.float32
    )


def body(out_grad, gate_act, up_act, gate_weight, up_weight, down_weight):
    hid_count = lax.axis_size("hid")
    gathered = lax.all_gather(out_grad, "hid", axis=0, tiled=True)
    rotated_grad = lax.psum_scatter(
        contract_rows(gathered, down_weight), "tok", scatter_dimension=0, tiled=True
    )
    current = rotated_grad
    position = lax.axis_index("hid")
    for level in range(hid_count.bit_length() - 1):
        partner = swapped(current, "hid", level)
        upper_half = position >> level & 1 == 1
        current = jnp.where(upper_half, partner - current, current + partner)
    hidden_grad = current * (1.0 / math.sqrt(hid_count))
    gate = gate_act.astype(jnp.float32)
    upper = up_act.astype(jnp.float32)
    logistic = jax.nn.sigmoid(gate)
    gate_grad = (hidden_grad * upper * logistic * (1.0 + gate * (1.0 - logistic))).astype(
        jnp.bfloat16
    )
    up_grad = (hidden_grad * gate * logistic).astype(jnp.bfloat16)
    gate_all, up_all = (
        lax.all_gather(gate_grad, "tok", axis=0, tiled=True),
        lax.all_gather(up_grad, "tok", axis=0, tiled=True),
    )
    summed = lax.psum_scatter(
        contract_rows(gate_all, gate_weight) + contract_rows(up_all, up_weight),
        "hid",
        scatter_dimension=0,
        tiled=True,
    )
    return summed.astype(jnp.bfloat16)


def solution(mesh):
    in_specs = (
        P("hid", "tok"),
        P("tok", "hid"),
        P("tok", "hid"),
        P("tok", "hid"),
        P("tok", "hid"),
        P("hid", "tok"),
    )
    out_specs = P("hid", "tok")
    return jax.shard_map(body, mesh=mesh, in_specs=in_specs, out_specs=out_specs, check_vma=False)
```

profile of v0, /device:TPU:0, one launch (start us, length us, event | category | flops | bytes accessed | tf_op | source)
XLA Modules:
  0.0 870.1 jit_solution(11427104828157271489)
XLA Ops:
  6.5 0.0 all-gather.4.cloned.1.call-start
  6.5 0.7 all-gather.4.cloned.1.call-update
  7.3 0.0 reduce-scatter.3.cloned.1.call-start
  7.3 41.4 %all-gather.4.cloned.1.call-done = bf16[1024,2048]{1,0:T(8,128)(2,1)} async-done(((bf16[128,2048]{1,0:T(8,128)(2,1)}), bf16[1024,2048]{1,0:T(8,128)(2,1)}) %all-gather.4.cloned.1.call-update) | async-done | bytes 4194320 | tf_op jit(solution)/shard_map/all_gather | solution.py:21
  48.7 22.8 %fusion.8 = f32[1024,3584]{1,0:T(8,128)} fusion(bf16[1024,2048]{1,0:T(8,128)(2,1)} %all-gather.4.cloned.1.call-done, bf16[3584,2048]{1,0:T(8,128)(2,1)} %param.11), kind=kOutput, calls=%fused_computation.15 | convolution fusion | flops 15032385536 | bytes 33554432 | tf_op jit(solution)/shard_map/dot_general | solution.py:14
  71.5 0.0 reduce-scatter.3.cloned.1.call-update
  71.6 0.0 all-gather.6.cloned.1.call-start
  71.6 245.8 %reduce-scatter.3.cloned.1.call-done = f32[256,3584]{1,0:T(8,128)} async-done(((f32[1024,3584]{1,0:T(8,128)}), f32[256,3584]{1,0:T(8,128)}) %reduce-scatter.3.cloned.1.call-update) | async-done | bytes 3670032 | tf_op jit(solution)/shard_map/reduce_scatter | solution.py:22
  317.4 0.0 collective-permute-start
  317.4 6.7 collective-permute-done
  324.2 5.6 add_select_fusion.1
  329.7 1.5 collective-permute-start.1
  331.2 0.0 copy-start
  331.2 80.2 %collective-permute-done.1 = f32[256,3584]{1,0:T(8,128)} collective-permute-done((f32[256,3584]{1,0:T(8,128)}, f32[256,3584]{1,0:T(8,128)}, u32[]{:S(2)}, u32[]{:S(2)}) %collective-permute-start.1) | collective-permute-done | bytes 3670048 | tf_op jit(solution)/shard_map/ppermute | solution.py:10
  411.4 5.6 add_select_fusion
  417.0 1.5 collective-permute-start.2
  418.5 79.4 %collective-permute-done.2 = f32[256,3584]{1,0:T(8,128)} collective-permute-done((f32[256,3584]{1,0:T(8,128)}, f32[256,3584]{1,0:T(8,128)}, u32[]{:S(2)}, u32[]{:S(2)}) %collective-permute-start.2) | collective-permute-done | bytes 3670048 | tf_op jit(solution)/shard_map/ppermute | solution.py:10
  497.8 0.0 copy-done
  497.8 6.0 fusion.7
  503.8 0.0 all-gather.6.cloned.1.call-update
  503.8 0.0 all-gather.8.cloned.1.call-start
  503.9 0.5 all-gather.8.cloned.1.call-update
  504.4 0.2 reduce-scatter.5.cloned.1.call-start
  504.6 132.9 %all-gather.6.cloned.1.call-done = bf16[1024,3584]{1,0:T(8,128)(2,1)} async-done(((bf16[256,3584]{1,0:T(8,128)(2,1)}), bf16[1024,3584]{1,0:T(8,128)(2,1)}) %all-gather.6.cloned.1.call-update) | async-done | bytes 7340048 | tf_op jit(solution)/shard_map/all_gather | solution.py:40
  637.5 21.5 %fusion.9 = f32[1024,2048]{1,0:T(8,128)} fusion(bf16[1024,3584]{1,0:T(8,128)(2,1)} %all-gather.6.cloned.1.call-done, bf16[2048,3584]{1,0:T(8,128)(2,1)} %param.9), kind=kOutput, calls=%fused_computation.16 | convolution fusion | flops 15032385536 | bytes 30408704 | tf_op jit(solution)/shard_map/dot_general | solution.py:14
  659.0 110.7 %all-gather.8.cloned.1.call-done = bf16[1024,3584]{1,0:T(8,128)(2,1)} async-done(((bf16[256,3584]{1,0:T(8,128)(2,1)}), bf16[1024,3584]{1,0:T(8,128)(2,1)}) %all-gather.8.cloned.1.call-update) | async-done | bytes 7340048 | tf_op jit(solution)/shard_map/all_gather | solution.py:41
  769.7 22.2 %convolution_add_fusion = f32[1024,2048]{1,0:T(8,128)} fusion(f32[1024,2048]{1,0:T(8,128)} %fusion.9, bf16[1024,3584]{1,0:T(8,128)(2,1)} %all-gather.8.cloned.1.call-done, bf16[2048,3584]{1,0:T(8,128)(2,1)} %param.10), kind=kOutput, calls=%fused_computation.3 | convolution fusion | flops 15034482688 | bytes 38797312 | tf_op jit(solution)/shard_map/dot_general | solution.py:14
  791.9 0.0 reduce-scatter.5.cloned.1.call-update
  791.9 69.6 %reduce-scatter.5.cloned.1.call-done = f32[128,2048]{1,0:T(8,128)} async-done(((f32[1024,2048]{1,0:T(8,128)}), f32[128,2048]{1,0:T(8,128)}) %reduce-scatter.5.cloned.1.call-update) | async-done | bytes 1048592 | tf_op jit(solution)/shard_map/reduce_scatter | solution.py:43
  861.5 2.1 convert_element_type.19
Async XLA Ops:
  6.5 42.2 %all-gather.4.cloned.1.call-start = ((), (), s32[]{:S(2)}) async-start(), calls=%async_computation.2 | async-start | bytes 4718592 | tf_op jit(solution)/shard_map/all_gather | solution.py:21
  7.3 310.2 %reduce-scatter.3.cloned.1.call-start = ((), (), s32[]{:S(2)}) async-start(), calls=%async_computation.3 | async-start | bytes 18350080 | tf_op jit(solution)/shard_map/reduce_scatter | solution.py:22
  71.6 565.9 %all-gather.6.cloned.1.call-start = ((), (), s32[]{:S(2)}) async-start(), calls=%async_computation.4 | async-start | bytes 9175040 | tf_op jit(solution)/shard_map/all_gather | solution.py:40
  317.4 6.8 collective-permute-start
  329.7 81.7 %collective-permute-start.1 = (f32[256,3584]{1,0:T(8,128)}, f32[256,3584]{1,0:T(8,128)}, u32[]{:S(2)}, u32[]{:S(2)}) collective-permute-start(f32[256,3584]{1,0:T(8,128)} %add_select_fusion.1), channel_id=1, source_target_pairs={{0,2},{1,3},{2,0},{3,1},{4,6},{5,7},{6,4},{7,5},{8,10},{9,11},{10,... | collective-permute-start | bytes 11010056 | tf_op jit(solution)/shard_map/ppermute | solution.py:10
  331.2 166.6 %copy-start = (bf16[256,3584]{1,0:T(8,128)(2,1)S(1)}, bf16[256,3584]{1,0:T(8,128)(2,1)}, u32[]{:S(2)}) copy-start(bf16[256,3584]{1,0:T(8,128)(2,1)} %param.7) | copy-start | bytes 5505028
  417.0 80.9 %collective-permute-start.2 = (f32[256,3584]{1,0:T(8,128)}, f32[256,3584]{1,0:T(8,128)}, u32[]{:S(2)}, u32[]{:S(2)}) collective-permute-start(f32[256,3584]{1,0:T(8,128)} %add_select_fusion), channel_id=1, source_target_pairs={{0,4},{1,5},{2,6},{3,7},{4,0},{5,1},{6,2},{7,3},{8,12},{9,13},{10,... | collective-permute-start | bytes 11010056 | tf_op jit(solution)/shard_map/ppermute | solution.py:10
  503.8 265.9 %all-gather.8.cloned.1.call-start = ((), (), s32[]{:S(2)}) async-start(), calls=%async_computation.5 | async-start | bytes 9175040 | tf_op jit(solution)/shard_map/all_gather | solution.py:41
  504.4 357.1 %reduce-scatter.5.cloned.1.call-start = ((), (), s32[]{:S(2)}) async-start(), calls=%async_computation.6 | async-start | bytes 9437184 | tf_op jit(solution)/shard_map/reduce_scatter | solution.py:43
Sparse Core Ops, SparseCore 0:
  9.2 39.4 all-gather.3
  71.7 245.6 reduce-scatter.2
  503.9 133.5 all-gather.5
  638.9 130.7 all-gather.7
  792.0 69.4 reduce-scatter.4
where the time goes:
time: 870 us
  waiting for transfers between devices  768 us (88%)
  matrix products  66.5 us (8%)
  other arithmetic  19.2 us (2%)
  between operations  13.1 us (2%)
    reduce_scatter x1, waiting for transfers between devices, body(): lax.psum_scatter(contract_rows(gathered, down_weight), 'tok', scatter_dim...  246 us
    ppermute x3, waiting for transfers between devices, swapped(): lax.ppermute(x, axis, [(i, i ^ 1 << bit) for i in range(lax.axis_size(axi...  166 us
    all_gather x1, waiting for transfers between devices, body(): lax.all_gather(gate_grad, 'tok', axis=0, tiled=True)  133 us
    all_gather x1, waiting for transfers between devices, body(): lax.all_gather(up_grad, 'tok', axis=0, tiled=True)  111 us
    reduce_scatter x1, waiting for transfers between devices, body(): lax.psum_scatter(contract_rows(gate_all, gate_weight) + contract_rows(up_...  69.6 us
    dot_general x3, matrix products, contract_rows(): lax.dot_general(left, right, (((1,), (1,)), ((), ())), preferred_element_...  66.5 us
    all_gather x1, waiting for transfers between devices, body(): gathered = lax.all_gather(out_grad, 'hid', axis=0, tiled=True)  41.4 us
  transfers between devices with their start and end apart: 8, of which 8 were waited for; matrix products, arithmetic and copies ran while one was open for 2% of the time, Pallas kernels for 0%

commit v1 on v0

v1 whole, which is shorter than its diff:
```python
import math

import jax
import jax.numpy as jnp
from jax import lax
from jax.sharding import PartitionSpec as P

CHUNKS = 4


def swapped(x, axis, bit):
    return lax.ppermute(x, axis, [(i, i ^ 1 << bit) for i in range(lax.axis_size(axis))])


def contract_rows(left, right):
    return lax.dot_general(
        left, right, (((1,), (1,)), ((), ())), preferred_element_type=jnp.float32
    )


def body(out_grad, gate_act, up_act, gate_weight, up_weight, down_weight):
    hid_count = lax.axis_size("hid")
    position = lax.axis_index("hid")
    gathered = lax.all_gather(out_grad, "hid", axis=0, tiled=True)
    width = down_weight.shape[0] // CHUNKS
    total = None
    for chunk in range(CHUNKS):
        cut = slice(chunk * width, (chunk + 1) * width)
        product = contract_rows(gathered, down_weight[cut]).astype(jnp.bfloat16)
        current = lax.psum_scatter(product, "tok", scatter_dimension=0, tiled=True)
        current = current.astype(jnp.float32)
        for level in range(hid_count.bit_length() - 1):
            sent = current if level == 0 else current.astype(jnp.bfloat16)
            partner = swapped(sent, "hid", level).astype(jnp.float32)
            upper_half = position >> level & 1 == 1
            current = jnp.where(upper_half, partner - current, current + partner)
        hidden_grad = current * (1.0 / math.sqrt(hid_count))
        gate = gate_act[:, cut].astype(jnp.float32)
        upper = up_act[:, cut].astype(jnp.float32)
        logistic = jax.nn.sigmoid(gate)
        gate_grad = (hidden_grad * upper * logistic * (1.0 + gate * (1.0 - logistic))).astype(
            jnp.bfloat16
        )
        up_grad = (hidden_grad * gate * logistic).astype(jnp.bfloat16)
        both = jnp.concatenate([gate_grad, up_grad], axis=1)
        both = lax.all_gather(both, "tok", axis=0, tiled=True)
        part = contract_rows(both[:, :width], gate_weight[:, cut]) + contract_rows(
            both[:, width:], up_weight[:, cut]
        )
        total = part if total is None else total + part
    summed = lax.psum_scatter(total, "hid", scatter_dimension=0, tiled=True)
    return summed.astype(jnp.bfloat16)


def solution(mesh):
    in_specs = (
        P("hid", "tok"),
        P("tok", "hid"),
        P("tok", "hid"),
        P("tok", "hid"),
        P("tok", "hid"),
        P("hid", "tok"),
    )
    out_specs = P("hid", "tok")
    return jax.shard_map(body, mesh=mesh, in_specs=in_specs, out_specs=out_specs, check_vma=False)
```

time: 870 us -> 633 us (0.73)
  waiting for transfers between devices: 768 us -> 438 us
  matrix products: 66.5 us -> 130 us
  other arithmetic: 19.2 us -> 29.7 us
    reduce_scatter x2 -> x5, waiting for transfers between devices: 315 us -> 151 us  [the longest x4 81.5 us: body(): current = lax.psum_scatter(product, 'tok', scatter_dimension=0, tiled=True)]
    ppermute x3 -> x12, waiting for transfers between devices: 166 us -> 55.3 us  [swapped(): lax.ppermute(x, axis, [(i, i ^ 1 << bit) for i in range(lax.axis_size(axi...]
    dot_general x3 -> x12, matrix products: 66.5 us -> 130 us  [contract_rows(): lax.dot_general(left, right, (((1,), (1,)), ((), ())), preferred_element_...]
    all_gather x2 -> x4, waiting for transfers between devices: 244 us -> 189 us  [body(): both = lax.all_gather(both, 'tok', axis=0, tiled=True)]
    convert_element_type x1 -> x14, other arithmetic: 5.96 us -> 22.5 us  [the longest x8 9.8 us: body(): sent = current if level == 0 else current.astype(jnp.bfloat16)]
    select_n x2 -> x0, other arithmetic: 11.1 us -> none  [body(): current = jnp.where(upper_half, partner - current, current + partner)]
  transfers between devices with their start and end apart: 8 -> 22, of which waited for: 8 -> 17; matrix products, arithmetic and copies ran while one was open for 2% -> 18% of each run, Pallas kernels for 0% -> 0%
where the time goes in v1:
time: 633 us; the launch traced here: 625 us
  waiting for transfers between devices  438 us (69%)
  matrix products  130 us (21%)
  other arithmetic  29.7 us (5%)
  between operations  14.1 us (2%)
  starting transfers between devices  11.9 us (2%)
    all_gather x4, waiting for transfers between devices, body(): both = lax.all_gather(both, 'tok', axis=0, tiled=True)  189 us
    dot_general x12, matrix products, contract_rows(): lax.dot_general(left, right, (((1,), (1,)), ((), ())), preferred_element_...  130 us
    reduce_scatter x4, waiting for transfers between devices, body(): current = lax.psum_scatter(product, 'tok', scatter_dimension=0, tiled=True)  81.5 us
    reduce_scatter x1, waiting for transfers between devices, body(): summed = lax.psum_scatter(total, 'hid', scatter_dimension=0, tiled=True)  70 us
    ppermute x12, waiting for transfers between devices, swapped(): lax.ppermute(x, axis, [(i, i ^ 1 << bit) for i in range(lax.axis_size(axi...  55.3 us
    all_gather x1, waiting for transfers between devices, body(): gathered = lax.all_gather(out_grad, 'hid', axis=0, tiled=True)  41.4 us
  transfers between devices with their start and end apart: 22, of which 17 were waited for; matrix products, arithmetic and copies ran while one was open for 18% of the time, Pallas kernels for 0%

profile of v1, /device:TPU:0, one launch (start us, length us, event | category | flops | bytes accessed | tf_op | source)
XLA Modules:
  0.0 624.5 jit_solution(14462643791718045105)
XLA Ops:
  7.3 41.4 %all-gather.6.cloned.1.call-done = bf16[1024,2048]{1,0:T(8,128)(2,1)} async-done(((bf16[128,2048]{1,0:T(8,128)(2,1)}), bf16[1024,2048]{1,0:T(8,128)(2,1)}) %all-gather.6.cloned.1.call-update) | async-done | bytes 4194320 | tf_op jit(solution)/shard_map/all_gather | solution.py:24
  48.7 9.1 %fusion.31 = bf16[1024,896]{1,0:T(8,128)(2,1)} fusion(bf16[1024,2048]{1,0:T(8,128)(2,1)} %all-gather.6.cloned.1.call-done, bf16[3584,2048]{1,0:T(8,128)(2,1)} %param.11), kind=kOutput, calls=%fused_computation.32 | convolution fusion | flops 3759013888 | bytes 9699328 | tf_op jit(solution)/shard_map/dot_general | solution.py:16
  57.9 9.1 %fusion.34 = bf16[1024,896]{1,0:T(8,128)(2,1)} fusion(bf16[1024,2048]{1,0:T(8,128)(2,1)} %all-gather.6.cloned.1.call-done, bf16[3584,2048]{1,0:T(8,128)(2,1)} %param.11), kind=kOutput, calls=%fused_computation.33 | convolution fusion | flops 3759013888 | bytes 9699328 | tf_op jit(solution)/shard_map/dot_general | solution.py:16
  67.0 9.1 %fusion.40 = bf16[1024,896]{1,0:T(8,128)(2,1)} fusion(bf16[1024,2048]{1,0:T(8,128)(2,1)} %all-gather.6.cloned.1.call-done, bf16[3584,2048]{1,0:T(8,128)(2,1)} %param.11), kind=kOutput, calls=%fused_computation.35 | convolution fusion | flops 3759013888 | bytes 9699328 | tf_op jit(solution)/shard_map/dot_general | solution.py:16
  76.4 9.1 %fusion.37 = bf16[1024,896]{1,0:T(8,128)(2,1)} fusion(bf16[1024,2048]{1,0:T(8,128)(2,1)} %all-gather.6.cloned.1.call-done, bf16[3584,2048]{1,0:T(8,128)(2,1)} %param.11), kind=kOutput, calls=%fused_computation.34 | convolution fusion | flops 3759013888 | bytes 9699328 | tf_op jit(solution)/shard_map/dot_general | solution.py:16
  85.6 11.8 %reduce-scatter.6.cloned.1.call-done = bf16[256,896]{1,0:T(8,128)(2,1)} async-done(((bf16[1024,896]{1,0:T(8,128)(2,1)}), bf16[256,896]{1,0:T(8,128)(2,1)}) %reduce-scatter.6.cloned.1.call-update) | async-done | bytes 458768 | tf_op jit(solution)/shard_map/reduce_scatter | solution.py:30
  97.4 2.2 convert_element_type.124
  99.6 38.8 %reduce-scatter.8.cloned.1.call-done = bf16[256,896]{1,0:T(8,128)(2,1)} async-done(((bf16[1024,896]{1,0:T(8,128)(2,1)}), bf16[256,896]{1,0:T(8,128)(2,1)}) %reduce-scatter.8.cloned.1.call-update) | async-done | bytes 458768 | tf_op jit(solution)/shard_map/reduce_scatter | solution.py:30
  138.3 2.1 convert_element_type.134
  146.5 9.4 %collective-permute-done.1 = bf16[256,896]{1,0:T(8,128)(2,1)S(1)} collective-permute-done((bf16[256,896]{1,0:T(8,128)(2,1)}, bf16[256,896]{1,0:T(8,128)(2,1)S(1)}, u32[]{:S(2)}, u32[]{:S(2)}) %collective-permute-start.1) | collective-permute-done | bytes 458784 | tf_op jit(solution)/shard_map/ppermute | solution.py:12
  158.4 7.0 %collective-permute-done.4 = bf16[256,896]{1,0:T(8,128)(2,1)} collective-permute-done((bf16[256,896]{1,0:T(8,128)(2,1)}, bf16[256,896]{1,0:T(8,128)(2,1)}, u32[]{:S(2)}, u32[]{:S(2)}) %collective-permute-start.4) | collective-permute-done | bytes 458784 | tf_op jit(solution)/shard_map/ppermute | solution.py:12
  169.1 10.9 %collective-permute-done.5 = bf16[256,896]{1,0:T(8,128)(2,1)} collective-permute-done((bf16[256,896]{1,0:T(8,128)(2,1)}, bf16[256,896]{1,0:T(8,128)(2,1)}, u32[]{:S(2)}, u32[]{:S(2)}) %collective-permute-start.5) | collective-permute-done | bytes 458784 | tf_op jit(solution)/shard_map/ppermute | solution.py:12
  180.0 4.4 fusion.60
  185.5 2.1 pad_maximum_fusion.1
  188.9 30.9 %reduce-scatter.10.cloned.1.call-done = bf16[256,896]{1,0:T(8,128)(2,1)} async-done(((bf16[1024,896]{1,0:T(8,128)(2,1)}), bf16[256,896]{1,0:T(8,128)(2,1)}) %reduce-scatter.10.cloned.1.call-update) | async-done | bytes 458768 | tf_op jit(solution)/shard_map/reduce_scatter | solution.py:30
  226.2 9.4 %collective-permute-done.10 = bf16[256,896]{1,0:T(8,128)(2,1)S(1)} collective-permute-done((bf16[256,896]{1,0:T(8,128)(2,1)S(1)}, bf16[256,896]{1,0:T(8,128)(2,1)S(1)}, u32[]{:S(2)}, u32[]{:S(2)}) %collective-permute-start.10) | collective-permute-done | bytes 458784 | tf_op jit(solution)/shard_map/ppermute | solution.py:12
  237.4 7.6 %collective-permute-done.7 = bf16[256,896]{1,0:T(8,128)(2,1)S(1)} collective-permute-done((bf16[256,896]{1,0:T(8,128)(2,1)S(1)}, bf16[256,896]{1,0:T(8,128)(2,1)S(1)}, u32[]{:S(2)}, u32[]{:S(2)}) %collective-permute-start.7) | collective-permute-done | bytes 458784 | tf_op jit(solution)/shard_map/ppermute | solution.py:12
  247.8 9.8 %collective-permute-done.8 = bf16[256,896]{1,0:T(8,128)(2,1)S(1)} collective-permute-done((bf16[256,896]{1,0:T(8,128)(2,1)S(1)}, bf16[256,896]{1,0:T(8,128)(2,1)S(1)}, u32[]{:S(2)}, u32[]{:S(2)}) %collective-permute-start.8) | collective-permute-done | bytes 458784 | tf_op jit(solution)/shard_map/ppermute | solution.py:12
  261.7 30.8 %all-gather.8.cloned.1.call-done = bf16[1024,1792]{1,0:T(8,128)(2,1)} async-done(((bf16[256,1792]{1,0:T(8,128)(2,1)}), bf16[1024,1792]{1,0:T(8,128)(2,1)}) %all-gather.8.cloned.1.call-update) | async-done | bytes 3670032 | tf_op jit(solution)/shard_map/all_gather | solution.py:46
  292.5 10.6 %fusion.17 = f32[1024,2048]{1,0:T(8,128)} fusion(bf16[2048,3584]{1,0:T(8,128)(2,1)} %param.10, bf16[1024,1792]{1,0:T(8,128)(2,1)} %all-gather.8.cloned.1.call-done), kind=kOutput, calls=%fused_computation.18 | convolution fusion | flops 3758096384 | bytes 13893632 | tf_op jit(solution)/shard_map/dot_general | solution.py:16
  303.1 8.7 %fusion.19 = f32[1024,2048]{1,0:T(8,128)} fusion(bf16[2048,3584]{1,0:T(8,128)(2,1)} %param.9, bf16[1024,1792]{1,0:T(8,128)(2,1)S(1)} %copy-done.7), kind=kOutput, calls=%fused_computation.20 | convolution fusion | flops 3758096384 | bytes 13893632 | tf_op jit(solution)/shard_map/dot_general | solution.py:16
  311.8 53.0 %all-gather.10.cloned.1.call-done = bf16[1024,1792]{1,0:T(8,128)(2,1)} async-done(((bf16[256,1792]{1,0:T(8,128)(2,1)}), bf16[1024,1792]{1,0:T(8,128)(2,1)}) %all-gather.10.cloned.1.call-update) | async-done | bytes 3670032 | tf_op jit(solution)/shard_map/all_gather | solution.py:46
  364.8 10.6 %fusion.11 = f32[1024,2048]{1,0:T(8,128)} fusion(bf16[2048,3584]{1,0:T(8,128)(2,1)} %param.10, bf16[1024,1792]{1,0:T(8,128)(2,1)} %all-gather.10.cloned.1.call-done), kind=kOutput, calls=%fused_computation.12 | convolution fusion | flops 3758096384 | bytes 13893632 | tf_op jit(solution)/shard_map/dot_general | solution.py:16
  375.4 8.8 %fusion.13 = f32[1024,2048]{1,0:T(8,128)} fusion(bf16[2048,3584]{1,0:T(8,128)(2,1)} %param.9, bf16[1024,1792]{1,0:T(8,128)(2,1)S(1)} %copy-done.8), kind=kOutput, calls=%fused_computation.14 | convolution fusion | flops 3758096384 | bytes 13893632 | tf_op jit(solution)/shard_map/dot_general | solution.py:16
  384.2 52.9 %all-gather.12.cloned.1.call-done = bf16[1024,1792]{1,0:T(8,128)(2,1)} async-done(((bf16[256,1792]{1,0:T(8,128)(2,1)}), bf16[1024,1792]{1,0:T(8,128)(2,1)}) %all-gather.12.cloned.1.call-update) | async-done | bytes 3670032 | tf_op jit(solution)/shard_map/all_gather | solution.py:46
  437.2 10.6 %fusion.5 = f32[1024,2048]{1,0:T(8,128)} fusion(bf16[2048,3584]{1,0:T(8,128)(2,1)} %param.10, bf16[1024,1792]{1,0:T(8,128)(2,1)} %all-gather.12.cloned.1.call-done), kind=kOutput, calls=%fused_computation.6 | convolution fusion | flops 3758096384 | bytes 13893632 | tf_op jit(solution)/shard_map/dot_general | solution.py:16
  447.8 9.0 %fusion.7 = f32[1024,2048]{1,0:T(8,128)} fusion(bf16[2048,3584]{1,0:T(8,128)(2,1)} %param.9, bf16[1024,1792]{1,0:T(8,128)(2,1)S(1)} %copy-done.9), kind=kOutput, calls=%fused_computation.8 | convolution fusion | flops 3758096384 | bytes 13893632 | tf_op jit(solution)/shard_map/dot_general | solution.py:16
  456.8 52.7 %all-gather.14.cloned.1.call-done = bf16[1024,1792]{1,0:T(8,128)(2,1)} async-done(((bf16[256,1792]{1,0:T(8,128)(2,1)}), bf16[1024,1792]{1,0:T(8,128)(2,1)}) %all-gather.14.cloned.1.call-update) | async-done | bytes 3670032 | tf_op jit(solution)/shard_map/all_gather | solution.py:46
  509.5 10.4 %fusion.1 = f32[1024,2048]{1,0:T(8,128)} fusion(bf16[2048,3584]{1,0:T(8,128)(2,1)} %param.9, bf16[1024,1792]{1,0:T(8,128)(2,1)} %all-gather.14.cloned.1.call-done), kind=kOutput, calls=%fused_computation.2 | convolution fusion | flops 3758096384 | bytes 13893632 | tf_op jit(solution)/shard_map/dot_general | solution.py:16
  519.9 25.3 %add_add_fusion = f32[1024,2048]{1,0:T(8,128)} fusion(f32[1024,2048]{1,0:T(8,128)} %fusion.1, f32[1024,2048]{1,0:T(8,128)} %fusion.7, f32[1024,2048]{1,0:T(8,128)} %fusion.5, f32[1024,2048]{1,0:T(8,128)} %fusion.13, f32[1024,2048]{1,0:T(8,128)} %fusion.11, f32[1024,2048]{1,0:T(8,128)} %fusion.19, f32[1024,2048]{1,0:T(8,128)} %fusion.17, ...), kind=kOutput, calls=%fused_computation | convolution fusion | flops 3772776448 | bytes 72613888 | tf_op jit(solution)/shard_map/dot_general | solution.py:16
  545.1 70.0 %reduce-scatter.14.cloned.1.call-done = f32[128,2048]{1,0:T(8,128)} async-done(((f32[1024,2048]{1,0:T(8,128)}), f32[128,2048]{1,0:T(8,128)}) %reduce-scatter.14.cloned.1.call-update) | async-done | bytes 1048592 | tf_op jit(solution)/shard_map/reduce_scatter | solution.py:51
  615.2 2.1 convert_element_type.163
  (73 shorter events, 30.7 us)
Async XLA Ops:
  6.5 42.2 %all-gather.6.cloned.1.call-start = ((), (), s32[]{:S(2)}) async-start(), calls=%async_computation.5 | async-start | bytes 4718592 | tf_op jit(solution)/shard_map/all_gather | solution.py:24
  7.3 90.2 %reduce-scatter.6.cloned.1.call-start = ((), (), s32[]{:S(2)}) async-start(), calls=%async_computation.6 | async-start | bytes 2293760 | tf_op jit(solution)/shard_map/reduce_scatter | solution.py:30
  57.8 80.5 %reduce-scatter.8.cloned.1.call-start = ((), (), s32[]{:S(2)}) async-start(), calls=%async_computation.8 | async-start | bytes 2293760 | tf_op jit(solution)/shard_map/reduce_scatter | solution.py:30
  67.0 120.7 %reduce-scatter.12.cloned.1.call-start = ((), (), s32[]{:S(2)}) async-start(), calls=%async_computation.12 | async-start | bytes 2293760 | tf_op jit(solution)/shard_map/reduce_scatter | solution.py:30
  76.2 143.6 %reduce-scatter.10.cloned.1.call-start = ((), (), s32[]{:S(2)}) async-start(), calls=%async_computation.10 | async-start | bytes 2293760 | tf_op jit(solution)/shard_map/reduce_scatter | solution.py:30
  85.6 206.9 %all-gather.8.cloned.1.call-start = ((), (), s32[]{:S(2)}) async-start(), calls=%async_computation.7 | async-start | bytes 4587520 | tf_op jit(solution)/shard_map/all_gather | solution.py:46
  97.4 58.5 %copy-start.2 = (bf16[256,896]{1,0:T(8,128)(2,1)S(1)}, bf16[256,896]{1,0:T(8,128)(2,1)}, u32[]{:S(2)}) copy-start(bf16[256,896]{1,0:T(8,128)(2,1)} %reduce-scatter.6.cloned.1.call-done) | copy-start | bytes 1376260
  99.6 40.9 %collective-permute-start = (f32[256,896]{1,0:T(8,128)}, f32[256,896]{1,0:T(8,128)S(1)}, u32[]{:S(2)}, u32[]{:S(2)}) collective-permute-start(f32[256,896]{1,0:T(8,128)} %convert_element_type.124), channel_id=1, source_target_pairs={{0,1},{1,0},{2,3},{3,2},{4,5},{5,4},{6,7},{7,6},{8,9},{9,8},{10,11... | collective-permute-start | bytes 2752520 | tf_op jit(solution)/shard_map/ppermute | solution.py:12
  138.3 27.1 %copy-start.3 = (bf16[256,896]{1,0:T(8,128)(2,1)S(1)}, bf16[256,896]{1,0:T(8,128)(2,1)}, u32[]{:S(2)}) copy-start(bf16[256,896]{1,0:T(8,128)(2,1)} %reduce-scatter.8.cloned.1.call-done) | copy-start | bytes 1376260
  140.4 3.4 collective-permute-start.3
  142.4 13.5 %collective-permute-start.1 = (bf16[256,896]{1,0:T(8,128)(2,1)}, bf16[256,896]{1,0:T(8,128)(2,1)S(1)}, u32[]{:S(2)}, u32[]{:S(2)}) collective-permute-start(bf16[256,896]{1,0:T(8,128)(2,1)} %fusion.91), channel_id=1, source_target_pairs={{0,2},{1,3},{2,0},{3,1},{4,6},{5,7},{6,4},{7,5},{8,10},{9,11},{10,... | collective-permute-start | bytes 1376264 | tf_op jit(solution)/shard_map/ppermute | solution.py:12
  145.7 19.7 %collective-permute-start.4 = (bf16[256,896]{1,0:T(8,128)(2,1)}, bf16[256,896]{1,0:T(8,128)(2,1)}, u32[]{:S(2)}, u32[]{:S(2)}) collective-permute-start(bf16[256,896]{1,0:T(8,128)(2,1)} %fusion.92), channel_id=1, source_target_pairs={{0,2},{1,3},{2,0},{3,1},{4,6},{5,7},{6,4},{7,5},{8,10},{9,11},{10,... | collective-permute-start | bytes 1376264 | tf_op jit(solution)/shard_map/ppermute | solution.py:12
  155.9 13.2 %copy-start.6 = (bf16[256,896]{1,0:T(8,128)(2,1)}, bf16[256,896]{1,0:T(8,128)(2,1)S(1)}, u32[]{:S(2)}) copy-start(bf16[256,896]{1,0:T(8,128)(2,1)S(1)} %collective-permute-done.1) | copy-start | bytes 1376260
  156.9 12.2 %collective-permute-start.2 = (bf16[256,896]{1,0:T(8,128)(2,1)}, bf16[256,896]{1,0:T(8,128)(2,1)}, u32[]{:S(2)}, u32[]{:S(2)}) collective-permute-start(bf16[256,896]{1,0:T(8,128)(2,1)} %fusion.90), channel_id=1, source_target_pairs={{0,4},{1,5},{2,6},{3,7},{4,0},{5,1},{6,2},{7,3},{8,12},{9,13},{10,... | collective-permute-start | bytes 1376264 | tf_op jit(solution)/shard_map/ppermute | solution.py:12
  167.5 12.5 %collective-permute-start.5 = (bf16[256,896]{1,0:T(8,128)(2,1)}, bf16[256,896]{1,0:T(8,128)(2,1)}, u32[]{:S(2)}, u32[]{:S(2)}) collective-permute-start(bf16[256,896]{1,0:T(8,128)(2,1)} %fusion.89), channel_id=1, source_target_pairs={{0,4},{1,5},{2,6},{3,7},{4,0},{5,1},{6,2},{7,3},{8,12},{9,13},{10,... | collective-permute-start | bytes 1376264 | tf_op jit(solution)/shard_map/ppermute | solution.py:12
  185.4 179.4 %all-gather.10.cloned.1.call-start = ((), (), s32[]{:S(2)}) async-start(), calls=%async_computation.9 | async-start | bytes 4587520 | tf_op jit(solution)/shard_map/all_gather | solution.py:46
  187.6 249.6 %all-gather.12.cloned.1.call-start = ((), (), s32[]{:S(2)}) async-start(), calls=%async_computation.11 | async-start | bytes 4587520 | tf_op jit(solution)/shard_map/all_gather | solution.py:46
  187.7 47.9 %copy-start = (bf16[256,896]{1,0:T(8,128)(2,1)S(1)}, bf16[256,896]{1,0:T(8,128)(2,1)}, u32[]{:S(2)}) copy-start(bf16[256,896]{1,0:T(8,128)(2,1)} %reduce-scatter.12.cloned.1.call-done) | copy-start | bytes 1376260
  188.8 32.2 %collective-permute-start.9 = (f32[256,896]{1,0:T(8,128)S(1)}, f32[256,896]{1,0:T(8,128)S(1)}, u32[]{:S(2)}, u32[]{:S(2)}) collective-permute-start(f32[256,896]{1,0:T(8,128)S(1)} %convert_element_type.154), channel_id=1, source_target_pairs={{0,1},{1,0},{2,3},{3,2},{4,5},{5,4},{6,7},{7,6},{8,9},{9,8},{10,11... | collective-permute-start | bytes 2752520 | tf_op jit(solution)/shard_map/ppermute | solution.py:12
  219.8 25.2 %copy-start.1 = (bf16[256,896]{1,0:T(8,128)(2,1)S(1)}, bf16[256,896]{1,0:T(8,128)(2,1)}, u32[]{:S(2)}) copy-start(bf16[256,896]{1,0:T(8,128)(2,1)} %reduce-scatter.10.cloned.1.call-done) | copy-start | bytes 1376260
  221.0 2.8 collective-permute-start.6
  222.2 35.4 %copy-start.4 = (bf16[256,3584]{1,0:T(8,128)(2,1)S(1)}, bf16[256,3584]{1,0:T(8,128)(2,1)}, u32[]{:S(2)}) copy-start(bf16[256,3584]{1,0:T(8,128)(2,1)} %param.8) | copy-start | bytes 5505028
  222.2 35.4 %copy-start.5 = (bf16[256,3584]{1,0:T(8,128)(2,1)S(1)}, bf16[256,3584]{1,0:T(8,128)(2,1)}, u32[]{:S(2)}) copy-start(bf16[256,3584]{1,0:T(8,128)(2,1)} %param.7) | copy-start | bytes 5505028
  222.2 13.4 %collective-permute-start.10 = (bf16[256,896]{1,0:T(8,128)(2,1)S(1)}, bf16[256,896]{1,0:T(8,128)(2,1)S(1)}, u32[]{:S(2)}, u32[]{:S(2)}) collective-permute-start(bf16[256,896]{1,0:T(8,128)(2,1)S(1)} %fusion.94), channel_id=1, source_target_pairs={{0,2},{1,3},{2,0},{3,1},{4,6},{5,7},{6,4},{7,5},{8,10},{9,11},{10,... | collective-permute-start | bytes 1376264 | tf_op jit(solution)/shard_map/ppermute | solution.py:12
  224.9 20.1 %collective-permute-start.7 = (bf16[256,896]{1,0:T(8,128)(2,1)S(1)}, bf16[256,896]{1,0:T(8,128)(2,1)S(1)}, u32[]{:S(2)}, u32[]{:S(2)}) collective-permute-start(bf16[256,896]{1,0:T(8,128)(2,1)S(1)} %fusion.93), channel_id=1, source_target_pairs={{0,2},{1,3},{2,0},{3,1},{4,6},{5,7},{6,4},{7,5},{8,10},{9,11},{10,... | collective-permute-start | bytes 1376264 | tf_op jit(solution)/shard_map/ppermute | solution.py:12
  235.9 11.9 %collective-permute-start.11 = (bf16[256,896]{1,0:T(8,128)(2,1)S(1)}, bf16[256,896]{1,0:T(8,128)(2,1)S(1)}, u32[]{:S(2)}, u32[]{:S(2)}) collective-permute-start(bf16[256,896]{1,0:T(8,128)(2,1)S(1)} %fusion.87), channel_id=1, source_target_pairs={{0,4},{1,5},{2,6},{3,7},{4,0},{5,1},{6,2},{7,3},{8,12},{9,13},{10,... | collective-permute-start | bytes 1376264 | tf_op jit(solution)/shard_map/ppermute | solution.py:12
  245.3 12.3 %collective-permute-start.8 = (bf16[256,896]{1,0:T(8,128)(2,1)S(1)}, bf16[256,896]{1,0:T(8,128)(2,1)S(1)}, u32[]{:S(2)}, u32[]{:S(2)}) collective-permute-start(bf16[256,896]{1,0:T(8,128)(2,1)S(1)} %fusion.88), channel_id=1, source_target_pairs={{0,4},{1,5},{2,6},{3,7},{4,0},{5,1},{6,2},{7,3},{8,12},{9,13},{10,... | collective-permute-start | bytes 1376264 | tf_op jit(solution)/shard_map/ppermute | solution.py:12
  260.4 249.1 %all-gather.14.cloned.1.call-start = ((), (), s32[]{:S(2)}) async-start(), calls=%async_computation.13 | async-start | bytes 4587520 | tf_op jit(solution)/shard_map/all_gather | solution.py:46
  261.5 353.7 %reduce-scatter.14.cloned.1.call-start = ((), (), s32[]{:S(2)}) async-start(), calls=%async_computation.14 | async-start | bytes 9437184 | tf_op jit(solution)/shard_map/reduce_scatter | solution.py:51
  292.5 10.6 %copy-start.7 = (bf16[1024,1792]{1,0:T(8,128)(2,1)S(1)}, bf16[1024,1792]{1,0:T(8,128)(2,1)}, u32[]{:S(2)}) copy-start(bf16[1024,1792]{1,0:T(8,128)(2,1)} %all-gather.8.cloned.1.call-done) | copy-start | bytes 11010052
  364.8 10.6 %copy-start.8 = (bf16[1024,1792]{1,0:T(8,128)(2,1)S(1)}, bf16[1024,1792]{1,0:T(8,128)(2,1)}, u32[]{:S(2)}) copy-start(bf16[1024,1792]{1,0:T(8,128)(2,1)} %all-gather.10.cloned.1.call-done) | copy-start | bytes 11010052
  437.2 10.6 %copy-start.9 = (bf16[1024,1792]{1,0:T(8,128)(2,1)S(1)}, bf16[1024,1792]{1,0:T(8,128)(2,1)}, u32[]{:S(2)}) copy-start(bf16[1024,1792]{1,0:T(8,128)(2,1)} %all-gather.12.cloned.1.call-done) | copy-start | bytes 11010052
Sparse Core Ops, SparseCore 0:
  9.2 39.4 all-gather.5
  58.0 39.4 reduce-scatter.5
  99.7 38.5 reduce-scatter.7
  140.5 38.5 reduce-scatter.11
  181.2 38.5 reduce-scatter.9
  221.2 71.2 all-gather.7
  294.1 70.7 all-gather.9
  366.4 70.7 all-gather.11
  438.7 70.7 all-gather.13
  545.3 69.8 reduce-scatter.13

commit v2 on v1

v2 whole, which is shorter than its diff:
```python
import functools
import math

import jax
import jax.numpy as jnp
from jax import lax
from jax.experimental import pallas as pl
from jax.experimental.pallas import tpu as pltpu
from jax.sharding import PartitionSpec as P

BF16, F32 = jnp.bfloat16, jnp.float32
MESH = pl.DeviceIdType.MESH


def dot_rows(left, right):
    return lax.dot_general(left, right, (((1,), (1,)), ((), ())), preferred_element_type=F32)


def kernel(
    Z, L, N, w, rows,
    x_ref, ga_ref, ua_ref, gw_hbm, uw_hbm, dw_hbm, acc,
    part, rs, mix0, mixn, cur, msend, grads, dwb, wb,
    rs_send, rs_recv, mix_send, mix_recv, ag_up, ag_dn, ag_recv, dw_sem, gw_sem, uw_sem,
):
    z = lax.axis_index("tok")
    hid = lax.axis_index("hid")
    last = Z - 1
    half = rows // 2
    base = last + L
    steps = N + base + last
    order = [list(range(L)), [0] + list(range(L - 1, 0, -1))]

    def bit_of(bit):
        return (hid // (1 << bit)) % 2

    def partner_of(bit):
        return hid + (1 - 2 * bit_of(bit)) * (1 << bit)

    def remote(src, dst, send, recv, **where):
        return pltpu.make_async_remote_copy(
            src_ref=src, dst_ref=dst, send_sem=send, recv_sem=recv,
            device_id=where, device_id_type=MESH,
        )

    def rs_copy(c, slot, to):
        return remote(rs.at[c, slot], rs.at[c, slot], rs_send.at[c, slot], rs_recv.at[c, slot], tok=to)

    def mix_copy(c, l, h):
        at = pl.ds(h * half, half)
        to = partner_of(order[h][l])
        if l == 0:
            src, dst = cur.at[0, at], mix0.at[c, at]
        else:
            src, dst = msend.at[l - 1, at], mixn.at[c, l - 1, at]
        return remote(src, dst, mix_send.at[l, h], mix_recv.at[c, l, h], hid=to)

    def ag_copy(c, b, to, sems):
        return remote(grads.at[c, b], grads.at[c, b], sems.at[c, b], ag_recv.at[c, b], tok=to)

    def dw_fetch(c):
        return pltpu.make_async_copy(
            dw_hbm.at[pl.ds(pl.multiple_of(c * w, w), w)], dwb.at[c % 2], dw_sem.at[c % 2])

    def gw_fetch(c):
        at = pl.ds(pl.multiple_of(c * w, w), w)
        return pltpu.make_async_copy(gw_hbm.at[:, at], wb.at[c % 2, :, pl.ds(0, w)], gw_sem.at[c % 2])

    def uw_fetch(c):
        at = pl.ds(pl.multiple_of(c * w, w), w)
        return pltpu.make_async_copy(uw_hbm.at[:, at], wb.at[c % 2, :, pl.ds(w, w)], uw_sem.at[c % 2])

    def within(c):
        return (c >= 0) & (c < N)

    def product(c):
        dw_fetch(c).wait()

        @pl.loop(0, Z)
        def _(b):
            at = pl.ds(pl.multiple_of(b * rows, rows), rows)
            part[c % Z, b] = dot_rows(x_ref[at, :], dwb[c % 2])

    barrier = pltpu.get_barrier_semaphore()

    @pl.when(z > 0)
    def _():
        pl.semaphore_signal(barrier, inc=1, device_id={"tok": z - 1}, device_id_type=MESH)

    @pl.when(z < last)
    def _():
        pl.semaphore_signal(barrier, inc=1, device_id={"tok": z + 1}, device_id_type=MESH)

    for bit in range(L):
        pl.semaphore_signal(barrier, inc=1, device_id={"hid": partner_of(bit)}, device_id_type=MESH)
    dw_fetch(0).start()
    dw_fetch(1).start()
    gw_fetch(0).start()
    uw_fetch(0).start()
    acc[...] = jnp.zeros_like(acc)
    pl.semaphore_wait(barrier, L + jnp.where(z > 0, 1, 0) + jnp.where(z < last, 1, 0))

    product(0)

    def combined(c, l):
        halves = []
        for h in (0, 1):
            copy = mix_copy(c, l, h)
            copy.wait_send()
            copy.wait_recv()
            at = pl.ds(h * half, half)
            got = mix0[c, at, :] if l == 0 else mixn[c, l - 1, at, :].astype(F32)
            sign = jnp.where(bit_of(order[h][l]) == 1, -1.0, 1.0).astype(F32)
            halves.append(cur[l, at, :] * sign + got)
        return halves

    @pl.loop(0, steps)
    def _(t):
        for k in range(last, 0, -1):
            c = t - base - k

            @pl.when(within(c) & (z - k >= 0))
            def _():
                b = z - k
                ag_copy(c, b, z, ag_up).wait_recv()

                @pl.when(z < last)
                def _():
                    ag_copy(c, b, z + 1, ag_up).start()

            @pl.when(within(c) & (z + k <= last))
            def _():
                b = z + k
                ag_copy(c, b, z, ag_dn).wait_recv()

                @pl.when(z > 0)
                def _():
                    ag_copy(c, b, z - 1, ag_dn).start()

        ce = t - base

        @pl.when(within(ce))
        def _():
            got = combined(ce, L - 1)
            for h in (0, 1):
                at = pl.ds(h * half, half)
                cols = pl.ds(pl.multiple_of(ce * w, w), w)
                hidden = got[h] * (1.0 / math.sqrt(1 << L))
                gate = ga_ref[at, cols].astype(F32)
                upper = ua_ref[at, cols].astype(F32)
                logistic = jax.nn.sigmoid(gate)
                scaled = hidden * logistic
                grads[ce, z, at, pl.ds(0, w)] = (
                    scaled * upper * (1.0 + gate * (1.0 - logistic))).astype(BF16)
                grads[ce, z, at, pl.ds(w, w)] = (scaled * gate).astype(BF16)

            @pl.when(z < last)
            def _():
                ag_copy(ce, z, z + 1, ag_up).start()

            @pl.when(z > 0)
            def _():
                ag_copy(ce, z, z - 1, ag_dn).start()

        for l in range(L - 1, 0, -1):
            cm = t - last - l

            @pl.when(within(cm))
            def _(l=l, cm=cm):
                got = combined(cm, l - 1)
                for h in (0, 1):
                    at = pl.ds(h * half, half)
                    cur[l, at, :] = got[h]
                    msend[l - 1, at, :] = got[h].astype(BF16)
                    mix_copy(cm, l, h).start()

        co = t - last

        @pl.when(within(co))
        def _():
            cur[0] = part[co % Z, z]

            @pl.when(z > 0)
            def _():
                rs_copy(co, z + 1, z).wait_recv()
                cur[0] += rs[co, z + 1].astype(F32)

            @pl.when(z < last)
            def _():
                rs_copy(co, z, z).wait_recv()
                cur[0] += rs[co, z].astype(F32)

            for h in (0, 1):
                mix_copy(co, 0, h).start()

        cu = t - z

        @pl.when(within(cu))
        def _():
            for b in range(Z - 1, 0, -1):
                @pl.when((b > z) & (z > 0))
                def _(b=b):
                    rs_copy(cu, b + 1, z).wait_recv()
                    rs[cu, b + 1] = (rs[cu, b + 1].astype(F32) + part[cu % Z, b]).astype(BF16)

                @pl.when((b > z) & (z == 0))
                def _(b=b):
                    rs[cu, b + 1] = part[cu % Z, b].astype(BF16)

                @pl.when(b > z)
                def _(b=b):
                    rs_copy(cu, b + 1, z + 1).start()

        cd = t - (last - z)

        @pl.when(within(cd))
        def _():
            for b in range(0, Z - 1):
                @pl.when((b < z) & (z < last))
                def _(b=b):
                    rs_copy(cd, b, z).wait_recv()
                    rs[cd, b] = (rs[cd, b].astype(F32) + part[cd % Z, b]).astype(BF16)

                @pl.when((b < z) & (z == last))
                def _(b=b):
                    rs[cd, b] = part[cd % Z, b].astype(BF16)

                @pl.when(b < z)
                def _(b=b):
                    rs_copy(cd, b, z - 1).start()

        c2 = t - base - last

        @pl.when(within(c2))
        def _():
            gw_fetch(c2).wait()
            uw_fetch(c2).wait()

            @pl.when(c2 + 1 < N)
            def _():
                gw_fetch(c2 + 1).start()
                uw_fetch(c2 + 1).start()

            width = acc.shape[1]
            tile = min(512, width)

            @pl.loop(0, Z)
            def _(b):
                at = pl.ds(pl.multiple_of(b * rows, rows), rows)
                for n in range(width // tile):
                    cols = pl.ds(n * tile, tile)
                    acc[at, cols] += dot_rows(grads[c2, b], wb[c2 % 2, cols, :])

        @pl.when(t + 1 < N)
        def _():
            @pl.when(t + 2 < N)
            def _():
                dw_fetch(t + 2).start()

            product(t + 1)

    @pl.loop(0, N)
    def _(c):
        for b in range(Z):
            @pl.when(b > z)
            def _():
                rs_copy(c, b + 1, z).wait_send()

            @pl.when(b < z)
            def _():
                rs_copy(c, b, z).wait_send()

            @pl.when((b <= z) & (z < last))
            def _():
                ag_copy(c, b, z, ag_up).wait_send()

            @pl.when((b >= z) & (z > 0))
            def _():
                ag_copy(c, b, z, ag_dn).wait_send()


def mixed_products(gathered, gate_act, up_act, gate_weight, up_weight, down_weight):
    Z, hids = lax.axis_size("tok"), lax.axis_size("hid")
    L = hids.bit_length() - 1
    rows, hidden = gate_act.shape
    w = 256 if hidden % 256 == 0 else 128
    N = hidden // w
    tokens, depth = gathered.shape
    vmem, hbm = pl.BlockSpec(memory_space=pltpu.VMEM), pl.BlockSpec(memory_space=pl.ANY)
    dma = pltpu.SemaphoreType.DMA
    flops = 6 * tokens * depth * hidden
    return pl.pallas_call(
        functools.partial(kernel, Z, L, N, w, rows),
        out_shape=jax.ShapeDtypeStruct((tokens, depth), F32),
        in_specs=[vmem, vmem, vmem, hbm, hbm, hbm],
        out_specs=vmem,
        scratch_shapes=[
            pltpu.VMEM((Z, Z, rows, w), F32),
            pltpu.VMEM((N, Z + 1, rows, w), BF16),
            pltpu.VMEM((N, rows, w), F32),
            pltpu.VMEM((N, L - 1, rows, w), BF16),
            pltpu.VMEM((L, rows, w), F32),
            pltpu.VMEM((L - 1, rows, w), BF16),
            pltpu.VMEM((N, Z, rows, 2 * w), BF16),
            pltpu.VMEM((2, w, depth), BF16),
            pltpu.VMEM((2, depth, 2 * w), BF16),
            dma((N, Z + 1)), dma((N, Z + 1)),
            dma((L, 2)), dma((N, L, 2)),
            dma((N, Z)), dma((N, Z)), dma((N, Z)),
            dma((2,)), dma((2,)), dma((2,)),
        ],
        compiler_params=pltpu.CompilerParams(
            collective_id=0, has_side_effects=True, vmem_limit_bytes=63 * 1024 * 1024),
        cost_estimate=pl.CostEstimate(
            flops=flops, bytes_accessed=6 * hidden * depth, transcendentals=rows * hidden),
    )(gathered, gate_act, up_act, gate_weight, up_weight, down_weight)


def body(out_grad, gate_act, up_act, gate_weight, up_weight, down_weight):
    gathered = lax.all_gather(out_grad, "hid", axis=0, tiled=True)
    total = mixed_products(gathered, gate_act, up_act, gate_weight, up_weight, down_weight)
    summed = lax.psum_scatter(total, "hid", scatter_dimension=0, tiled=True)
    return summed.astype(BF16)


def solution(mesh):
    in_specs = (
        P("hid", "tok"),
        P("tok", "hid"),
        P("tok", "hid"),
        P("tok", "hid"),
        P("tok", "hid"),
        P("hid", "tok"),
    )
    out_specs = P("hid", "tok")
    return jax.shard_map(body, mesh=mesh, in_specs=in_specs, out_specs=out_specs, check_vma=False)
```

time: 633 us -> 458 us (0.72); the launches traced: 625 us -> 458 us
  Pallas kernels: 0 us -> 332 us
  waiting for transfers between devices: 438 us -> 111 us
  matrix products: 130 us -> 0 us
  other arithmetic: 29.7 us -> 2.08 us
  starting transfers between devices: 11.9 us -> 0.04 us
    pallas_call x0 -> x1, Pallas kernels: none -> 332 us  [mixed_products(): pl.pallas_call(functools.partial(kernel, Z, L, N, w, rows), out_shape=jax...]
    all_gather x4 -> x0, waiting for transfers between devices: 189 us -> none  [body(): both = lax.all_gather(both, 'tok', axis=0, tiled=True)]
    dot_general x12 -> x0, matrix products: 130 us -> none  [contract_rows(): lax.dot_general(left, right, (((1,), (1,)), ((), ())), preferred_element_...]
    reduce_scatter x4 -> x0, waiting for transfers between devices: 81.5 us -> none  [body(): current = lax.psum_scatter(product, 'tok', scatter_dimension=0, tiled=True)]
    ppermute x12 -> x0, waiting for transfers between devices: 55.3 us -> none  [swapped(): lax.ppermute(x, axis, [(i, i ^ 1 << bit) for i in range(lax.axis_size(axi...]
    convert_element_type x15 -> x1, other arithmetic: 24.6 us -> 2.08 us  [body(): return summed.astype(BF16)]
    ppermute x12 -> x0, starting transfers between devices: 11.1 us -> none  [swapped(): lax.ppermute(x, axis, [(i, i ^ 1 << bit) for i in range(lax.axis_size(axi...]
  transfers between devices with their start and end apart: 22 -> 2, of which waited for: 17 -> 2; matrix products, arithmetic and copies ran while one was open for 18% -> 0% of each run, Pallas kernels for 0% -> 0%
where the time goes in v2:
time: 458 us
  Pallas kernels  332 us (72%)
  waiting for transfers between devices  111 us (24%)
  between operations  13.4 us (3%)
    pallas_call x1, Pallas kernels, mixed_products(): pl.pallas_call(functools.partial(kernel, Z, L, N, w, rows), out_shape=jax...  332 us
    reduce_scatter x1, waiting for transfers between devices, body(): summed = lax.psum_scatter(total, 'hid', scatter_dimension=0, tiled=True)  68.7 us
    all_gather x1, waiting for transfers between devices, body(): gathered = lax.all_gather(out_grad, 'hid', axis=0, tiled=True)  41.4 us
  transfers between devices with their start and end apart: 2, of which 2 were waited for; matrix products, arithmetic and copies ran while one was open for 0% of the time, Pallas kernels for 0%

profile of v2, /device:TPU:0, one launch (start us, length us, event | category | flops | bytes accessed | tf_op | source)
XLA Modules:
  0.0 458.2 jit_solution(6331896191131620363)
XLA Ops:
  6.5 0.0 all-gather.2.cloned.1.call-start
  6.5 0.7 all-gather.2.cloned.1.call-update
  7.3 0.0 reduce-scatter.2.cloned.1.call-start
  7.3 41.4 %all-gather.2.cloned.1.call-done.x_ref = bf16[1024,2048]{1,0:T(8,128)(2,1)} async-done(((bf16[128,2048]{1,0:T(8,128)(2,1)}), bf16[1024,2048]{1,0:T(8,128)(2,1)}) %all-gather.2.cloned.1.call-update) | async-done | bytes 4194320 | tf_op jit(solution)/shard_map/all_gather | solution.py:319
  48.7 331.9 %shard_map.64 = f32[1024,2048]{1,0:T(8,128)} custom-call(bf16[1024,2048]{1,0:T(8,128)(2,1)} %all-gather.2.cloned.1.call-done.x_ref, bf16[256,3584]{1,0:T(8,128)(2,1)} %ga_ref.1, bf16[256,3584]{1,0:T(8,128)(2,1)} %ua_ref.1, bf16[2048,3584]{1,0:T(8,128)(2,1)} %gw_hbm.1, bf16[2048,3584]{1,0:T(8,128)(2,1)} %uw_hbm.1, bf16[3584,2048]{1,0:T(8,128)(2,1)} %dw_hbm.1), custom_call_target="tpu_custom_call" | custom-call | flops 45097156608 | bytes 44040192 | tf_op jit(solution)/shard_map/pallas_call | solution.py:291
  380.6 0.0 reduce-scatter.2.cloned.1.call-update
  380.6 68.7 %reduce-scatter.2.cloned.1.call-done = f32[128,2048]{1,0:T(8,128)} async-done(((f32[1024,2048]{1,0:T(8,128)}), f32[128,2048]{1,0:T(8,128)}) %reduce-scatter.2.cloned.1.call-update) | async-done | bytes 1048592 | tf_op jit(solution)/shard_map/reduce_scatter | solution.py:321
  449.3 2.1 convert_element_type.3
Async XLA Ops:
  6.5 42.2 %all-gather.2.cloned.1.call-start = ((), (), s32[]{:S(2)}) async-start(), calls=%async_computation.1 | async-start | bytes 4718592 | tf_op jit(solution)/shard_map/all_gather | solution.py:319
  7.3 442.1 %reduce-scatter.2.cloned.1.call-start = ((), (), s32[]{:S(2)}) async-start(), calls=%async_computation.2 | async-start | bytes 9437184 | tf_op jit(solution)/shard_map/reduce_scatter | solution.py:321
Sparse Core Ops, SparseCore 0:
  9.2 39.4 all-gather.1
  380.7 68.5 reduce-scatter.1

commit v3 on v2

--- a/solution.py
+++ b/solution.py
@@ -12,15 +12,23 @@
 MESH = pl.DeviceIdType.MESH
 
 
+def subsets(items):
+    found = [()]
+    for item in items:
+        found += [one + (item,) for one in found]
+    return found
+
+
 def dot_rows(left, right):
     return lax.dot_general(left, right, (((1,), (1,)), ((), ())), preferred_element_type=F32)
 
 
 def kernel(
     Z, L, N, w, rows,
-    x_ref, ga_ref, ua_ref, gw_hbm, uw_hbm, dw_hbm, acc,
-    part, rs, mix0, mixn, cur, msend, grads, dwb, wb,
+    x_hbm, ga_ref, ua_ref, gw_hbm, uw_hbm, dw_hbm, out_ref,
+    xbuf, acc, stage, part, rs, mix0, mixn, cur, msend, grads, dwb, wb,
     rs_send, rs_recv, mix_send, mix_recv, ag_up, ag_dn, ag_recv, dw_sem, gw_sem, uw_sem,
+    own_sem, head_send, head_recv, tail_send, tail_recv,
 ):
     z = lax.axis_index("tok")
     hid = lax.axis_index("hid")
@@ -29,12 +37,21 @@
     base = last + L
     steps = N + base + last
     order = [list(range(L)), [0] + list(range(L - 1, 0, -1))]
+    head_order = [list(range(1, L)) + [0], list(range(L - 1, 0, -1)) + [0]]
+    block, width = x_hbm.shape
+    side = [pl.ds(h * (width // 2), width // 2) for h in (0, 1)]
 
     def bit_of(bit):
         return (hid // (1 << bit)) % 2
 
     def partner_of(bit):
         return hid + (1 - 2 * bit_of(bit)) * (1 << bit)
+
+    def rows_of(p):
+        return pl.ds(pl.multiple_of(p * block, block), block)
+
+    def flipped(bits):
+        return hid + sum((1 - 2 * bit_of(bit)) * (1 << bit) for bit in bits)
 
     def remote(src, dst, send, recv, **where):
         return pltpu.make_async_remote_copy(
@@ -57,6 +74,29 @@
     def ag_copy(c, b, to, sems):
         return remote(grads.at[c, b], grads.at[c, b], sems.at[c, b], ag_recv.at[c, b], tok=to)
 
+    def head_copies(h, s, arriving):
+        bit = head_order[h][s]
+        copies = []
+        for i, sub in enumerate(subsets(head_order[h][:s])):
+            idx = (1 << s) - 1 + i
+            at = xbuf.at[rows_of(flipped(sub + (bit,) if arriving else sub)), side[h]]
+            copies.append(remote(
+                at, at, head_send.at[h, idx], head_recv.at[h, idx], hid=partner_of(bit)))
+        return copies
+
+    def tail_steps(h, s):
+        bit, rest = order[h][s], order[h][s + 1:]
+        offset = (1 << L) - (1 << (L - s))
+        found = []
+        for i, sub in enumerate(subsets(rest)):
+            idx = offset + i
+            at = pl.ds(idx * block, block)
+            copy = remote(
+                stage.at[at, side[h]], xbuf.at[at, side[h]],
+                tail_send.at[h, idx], tail_recv.at[h, idx], hid=partner_of(bit))
+            found.append((flipped(sub), flipped(sub + (bit,)), at, copy))
+        return found
+
     def dw_fetch(c):
         return pltpu.make_async_copy(
             dw_hbm.at[pl.ds(pl.multiple_of(c * w, w), w)], dwb.at[c % 2], dw_sem.at[c % 2])
@@ -78,7 +118,7 @@
         @pl.loop(0, Z)
         def _(b):
             at = pl.ds(pl.multiple_of(b * rows, rows), rows)
-            part[c % Z, b] = dot_rows(x_ref[at, :], dwb[c % 2])
+            part[c % Z, b] = dot_rows(xbuf[at, :], dwb[c % 2])
 
     barrier = pltpu.get_barrier_semaphore()
 
@@ -92,13 +132,30 @@
 
     for bit in range(L):
         pl.semaphore_signal(barrier, inc=1, device_id={"hid": partner_of(bit)}, device_id_type=MESH)
+    own = pltpu.make_async_copy(x_hbm, xbuf.at[rows_of(hid)], own_sem)
+    own.start()
     dw_fetch(0).start()
     dw_fetch(1).start()
     gw_fetch(0).start()
     uw_fetch(0).start()
+    pl.semaphore_wait(barrier, L + jnp.where(z > 0, 1, 0) + jnp.where(z < last, 1, 0))
+
+    own.wait()
+    for s in range(L):
+        for h in (0, 1):
+            if s > 0:
+                for copy in head_copies(h, s - 1, True):
+                    copy.wait_recv()
+            for copy in head_copies(h, s, False):
+                copy.start()
     acc[...] = jnp.zeros_like(acc)
-    pl.semaphore_wait(barrier, L + jnp.where(z > 0, 1, 0) + jnp.where(z < last, 1, 0))
-
+    for h in (0, 1):
+        for copy in head_copies(h, L - 1, True):
+            copy.wait_recv()
+    for s in range(L):
+        for h in (0, 1):
+            for copy in head_copies(h, s, False):
+                copy.wait_send()
     product(0)
 
     def combined(c, l):
@@ -240,7 +297,6 @@
                 gw_fetch(c2 + 1).start()
                 uw_fetch(c2 + 1).start()
 
-            width = acc.shape[1]
             tile = min(512, width)
 
             @pl.loop(0, Z)
@@ -258,6 +314,26 @@
 
             product(t + 1)
 
+    def add_arrived(h, s):
+        for kept, _, at, copy in tail_steps(h, s):
+            copy.wait_recv()
+            acc[rows_of(kept), side[h]] += xbuf[at, side[h]].astype(F32)
+
+    for s in range(L):
+        for h in (0, 1):
+            if s > 0:
+                add_arrived(h, s - 1)
+            for _, sent, at, copy in tail_steps(h, s):
+                stage[at, side[h]] = acc[rows_of(sent), side[h]].astype(BF16)
+                copy.start()
+    for h in (0, 1):
+        add_arrived(h, L - 1)
+        out_ref[:, side[h]] = acc[rows_of(hid), side[h]].astype(BF16)
+    for s in range(L):
+        for h in (0, 1):
+            for _, _, _, copy in tail_steps(h, s):
+                copy.wait_send()
+
     @pl.loop(0, N)
     def _(c):
         for b in range(Z):
@@ -278,22 +354,26 @@
                 ag_copy(c, b, z, ag_dn).wait_send()
 
 
-def mixed_products(gathered, gate_act, up_act, gate_weight, up_weight, down_weight):
+def body(out_grad, gate_act, up_act, gate_weight, up_weight, down_weight):
     Z, hids = lax.axis_size("tok"), lax.axis_size("hid")
     L = hids.bit_length() - 1
     rows, hidden = gate_act.shape
     w = 256 if hidden % 256 == 0 else 128
     N = hidden // w
-    tokens, depth = gathered.shape
+    block, depth = out_grad.shape
+    tokens = hids * block
     vmem, hbm = pl.BlockSpec(memory_space=pltpu.VMEM), pl.BlockSpec(memory_space=pl.ANY)
     dma = pltpu.SemaphoreType.DMA
     flops = 6 * tokens * depth * hidden
     return pl.pallas_call(
         functools.partial(kernel, Z, L, N, w, rows),
-        out_shape=jax.ShapeDtypeStruct((tokens, depth), F32),
-        in_specs=[vmem, vmem, vmem, hbm, hbm, hbm],
+        out_shape=jax.ShapeDtypeStruct((block, depth), BF16),
+        in_specs=[hbm, vmem, vmem, hbm, hbm, hbm],
         out_specs=vmem,
         scratch_shapes=[
+            pltpu.VMEM((tokens, depth), BF16),
+            pltpu.VMEM((tokens, depth), F32),
+            pltpu.VMEM((tokens - block, depth), BF16),
             pltpu.VMEM((Z, Z, rows, w), F32),
             pltpu.VMEM((N, Z + 1, rows, w), BF16),
             pltpu.VMEM((N, rows, w), F32),
@@ -307,19 +387,13 @@
             dma((L, 2)), dma((N, L, 2)),
             dma((N, Z)), dma((N, Z)), dma((N, Z)),
             dma((2,)), dma((2,)), dma((2,)),
+            dma, dma((2, hids)), dma((2, hids)), dma((2, hids)), dma((2, hids)),
         ],
         compiler_params=pltpu.CompilerParams(
             collective_id=0, has_side_effects=True, vmem_limit_bytes=63 * 1024 * 1024),
         cost_estimate=pl.CostEstimate(
             flops=flops, bytes_accessed=6 * hidden * depth, transcendentals=rows * hidden),
-    )(gathered, gate_act, up_act, gate_weight, up_weight, down_weight)
-
-
-def body(out_grad, gate_act, up_act, gate_weight, up_weight, down_weight):
-    gathered = lax.all_gather(out_grad, "hid", axis=0, tiled=True)
-    total = mixed_products(gathered, gate_act, up_act, gate_weight, up_weight, down_weight)
-    summed = lax.psum_scatter(total, "hid", scatter_dimension=0, tiled=True)
-    return summed.astype(BF16)
+    )(out_grad, gate_act, up_act, gate_weight, up_weight, down_weight)
 
 
 def solution(mesh):

time: 458 us -> 380 us (0.83)
  waiting for transfers between devices: 111 us -> 0 us
  Pallas kernels: 332 us -> 378 us
  between operations: 13.4 us -> 0.01 us
    reduce_scatter x1 -> x0, waiting for transfers between devices: 68.7 us -> none  [body(): summed = lax.psum_scatter(total, 'hid', scatter_dimension=0, tiled=True)]
    pallas_call x1, Pallas kernels: 332 us -> 378 us  [body(): pl.pallas_call(functools.partial(kernel, Z, L, N, w, rows), out_shape=jax...]
    all_gather x1 -> x0, waiting for transfers between devices: 41.4 us -> none  [body(): gathered = lax.all_gather(out_grad, 'hid', axis=0, tiled=True)]
  transfers between devices with their start and end apart: 2 -> 0, of which waited for: 2 -> 0; matrix products, arithmetic and copies ran while one was open for 0% -> 0% of each run, Pallas kernels for 0% -> 0%
where the time goes in v3:
time: 380 us
  Pallas kernels  378 us (99%)
    pallas_call x1, Pallas kernels, body(): pl.pallas_call(functools.partial(kernel, Z, L, N, w, rows), out_shape=jax...  378 us

profile of v3, /device:TPU:0, one launch (start us, length us, event | category | flops | bytes accessed | tf_op | source)
XLA Modules:
  0.0 380.2 jit_solution(10503994561830070764)
XLA Ops:
  0.0 378.3 %shard_map.64 = bf16[128,2048]{1,0:T(8,128)(2,1)} custom-call(bf16[128,2048]{1,0:T(8,128)(2,1)} %x_hbm.1, bf16[256,3584]{1,0:T(8,128)(2,1)} %ga_ref.1, bf16[256,3584]{1,0:T(8,128)(2,1)} %ua_ref.1, bf16[2048,3584]{1,0:T(8,128)(2,1)} %gw_hbm.1, bf16[2048,3584]{1,0:T(8,128)(2,1)} %uw_hbm.1, bf16[3584,2048]{1,0:T(8,128)(2,1)} %dw_hbm.1), custom_call_target="tpu_custom_call" | custom-call | flops 45097156608 | bytes 44040192 | tf_op jit(solution)/shard_map/pallas_call | solution.py:368
  378.3 1.9 copy.8

commit v4 on v3

--- a/solution.py
+++ b/solution.py
@@ -358,7 +358,7 @@
     Z, hids = lax.axis_size("tok"), lax.axis_size("hid")
     L = hids.bit_length() - 1
     rows, hidden = gate_act.shape
-    w = 256 if hidden % 256 == 0 else 128
+    w = 128
     N = hidden // w
     block, depth = out_grad.shape
     tokens = hids * block

time: 380 us -> 363 us (0.955)
  Pallas kernels: 378 us -> 360 us
    pallas_call x1, Pallas kernels: 378 us -> 360 us  [body(): pl.pallas_call(functools.partial(kernel, Z, L, N, w, rows), out_shape=jax...]
where the time goes in v4:
time: 363 us; the launch traced here: 362 us
  Pallas kernels  360 us (99%)
    pallas_call x1, Pallas kernels, body(): pl.pallas_call(functools.partial(kernel, Z, L, N, w, rows), out_shape=jax...  360 us

profile of v4, /device:TPU:0, one launch (start us, length us, event | category | flops | bytes accessed | tf_op | source)
XLA Modules:
  0.0 362.2 jit_solution(15860437508117287983)
XLA Ops:
  0.0 360.3 %shard_map.64 = bf16[128,2048]{1,0:T(8,128)(2,1)} custom-call(bf16[128,2048]{1,0:T(8,128)(2,1)} %x_hbm.1, bf16[256,3584]{1,0:T(8,128)(2,1)} %ga_ref.1, bf16[256,3584]{1,0:T(8,128)(2,1)} %ua_ref.1, bf16[2048,3584]{1,0:T(8,128)(2,1)} %gw_hbm.1, bf16[2048,3584]{1,0:T(8,128)(2,1)} %uw_hbm.1, bf16[3584,2048]{1,0:T(8,128)(2,1)} %dw_hbm.1), custom_call_target="tpu_custom_call" | custom-call | flops 45097156608 | bytes 44040192 | tf_op jit(solution)/shard_map/pallas_call | solution.py:368
  360.3 1.9 copy.8
